TPU v7x, 512 devices: a whole 4x4x16 slice. The times are simulated.
512 devices in a mesh: section: 2 (over core), tp: 4 (over x), ep: 64 (over z, y).
Axes of the slice: x: 4, y: 4, z: 16, core: 2. Of those that a mesh axis runs over, the one named last changes fastest.
Arguments:
- tokens: bfloat16 [2, 4096, 2048], P(None, 'ep', 'tp'), may hold values from -12 to 12
- norm_gain: float32 [2, 2048], P('section'), may hold values from 0.1 to 1.9
- expert_gate: bfloat16 [2, 64, 2048, 1024], P('section', 'ep', None, 'tp'), may hold values from -0.125 to 0.125
- expert_up: bfloat16 [2, 64, 2048, 1024], P('section', 'ep', None, 'tp'), may hold values from -0.125 to 0.125
- expert_down: bfloat16 [2, 64, 1024, 2048], P('section', 'ep', 'tp'), may hold values from -0.1875 to 0.1875
- routes: int32 [2, 2, 4096, 8], P('section', None, 'ep'), may hold values from 0 to 63, all different within a row; in each aligned block of 64 rows (0 to 63, 64 to 127, ..., all dimensions but the last counted through in order) at most 9 rows name the same one
- route_weights: float32 [2, 2, 4096, 8], P('section', None, 'ep'), may hold values from 0.1 to 0.4
Outputs:
- layer_states: bfloat16 [2, 2, 4096, 2048], P('section', None, 'ep', 'tp')
Inputs may be any that keep to these rules, and one draw needn't show every extreme that they name: `routes`: in each layer and micro-batch, the 64 tokens of one index of ep name one expert at most 9 times, and this is reached; the experts of one token differ.
All inputs are finite; a program needn't handle non-finite values.
Results may differ from a plain program's by a relative error of at most 0.0075.
Values may be sent and summed in bfloat16 or wider, within the bound.
A program may use at most 64 MiB of HBM per device.

v0:
```python
import jax
import jax.numpy as jnp
from jax import lax
from jax.sharding import PartitionSpec as P

EPSILON = 1e-06


def from_behind(value, axis, by):
    count = lax.axis_size(axis)
    pairs = [(i, i + by) for i in range(count) if 0 <= i + by < count]
    return lax.ppermute(value, axis, pairs)


def shards(tokens, norm_gain, expert_gate, expert_up, expert_down, routes, route_weights):
    section_rank = lax.axis_index("section")
    section_total = lax.axis_size("section")
    tensor_rank = lax.axis_index("tp")
    tensor_count = lax.axis_size("tp")
    expert_count = lax.axis_size("ep")
    micro_count, token_count, quarter = tokens.shape
    width = quarter * tensor_count
    top_count = routes.shape[-1]
    capacity = max(2, token_count * top_count * 9 // (8 * expert_count))
    slot_total = expert_count * capacity
    gain_row = norm_gain[0]
    weight_gate = expert_gate[0, 0]
    weight_up = expert_up[0, 0]
    weight_down = expert_down[0, 0]
    received = jnp.zeros((token_count, quarter), jnp.bfloat16)
    results = jnp.zeros((micro_count, token_count, quarter), jnp.bfloat16)
    tick_total = micro_count + section_total - 1
    for step_number in range(tick_total):
        offset_micro = step_number - section_rank
        micro_index = jnp.clip(offset_micro, 0, micro_count - 1)
        current = jnp.where(section_rank == 0, tokens[min(step_number, micro_count - 1)], received)
        expert_ids = lax.dynamic_index_in_dim(routes[0], micro_index, 0, keepdims=False)
        weights = lax.dynamic_index_in_dim(route_weights[0], micro_index, 0, keepdims=False)
        flat_ids = expert_ids.reshape(-1)
        onehot = (flat_ids[:, None] == jnp.arange(expert_count, dtype=jnp.int32)[None, :]).astype(
            jnp.int32
        )
        position = jnp.sum((jnp.cumsum(onehot, axis=0) - onehot) * onehot, axis=1)
        slots = flat_ids * capacity + position
        placed = slots[None, :] == jnp.arange(slot_total, dtype=jnp.int32)[:, None]
        placed = placed.reshape(slot_total, token_count, top_count)
        spread = jnp.any(placed, axis=2).astype(jnp.bfloat16)
        values = current.astype(jnp.float32)
        square_sum = lax.psum(jnp.sum(values * values, axis=1), "tp")
        own_gain = lax.dynamic_slice_in_dim(gain_row, tensor_rank * quarter, quarter)
        scale = lax.rsqrt(square_sum / width + EPSILON)
        normed = (values * scale[:, None] * own_gain).astype(jnp.bfloat16)
        buffer = jnp.dot(spread, normed, preferred_element_type=jnp.float32).astype(jnp.bfloat16)
        arrived = lax.all_to_all(
            buffer.reshape(expert_count, capacity, quarter),
            "ep",
            split_axis=0,
            concat_axis=0,
            tiled=True,
        )
        shard_part = lax.all_gather(arrived, "tp", axis=2, tiled=True)
        feature_count = shard_part.shape[2]
        rows_part = shard_part.reshape(slot_total, feature_count)
        gate_act = jnp.dot(rows_part, weight_gate, preferred_element_type=jnp.float32)
        up_act = jnp.dot(rows_part, weight_up, preferred_element_type=jnp.float32)
        hidden = (jax.nn.silu(gate_act) * up_act).astype(jnp.bfloat16)
        partial_value = jnp.dot(hidden, weight_down, preferred_element_type=jnp.float32).astype(
            jnp.bfloat16
        )
        grouped = lax.all_to_all(
            partial_value.reshape(slot_total, tensor_count, quarter),
            "tp",
            split_axis=1,
            concat_axis=1,
            tiled=True,
        )
        expert_out = jnp.sum(grouped.astype(jnp.float32), axis=1).astype(jnp.bfloat16)
        returned = lax.all_to_all(
            expert_out.reshape(expert_count, capacity, quarter),
            "ep",
            split_axis=0,
            concat_axis=0,
            tiled=True,
        )
        picked = jnp.take(returned.reshape(slot_total, quarter), slots, axis=0)
        picked = picked.reshape(token_count, top_count, quarter)
        combined = jnp.einsum(
            "tk,tkd->td", weights, picked.astype(jnp.float32), precision=lax.Precision.HIGHEST
        )
        output_rows = (values + combined).astype(jnp.bfloat16)
        active = (offset_micro >= 0) & (offset_micro < micro_count)
        previous = lax.dynamic_index_in_dim(results, micro_index, 0, keepdims=False)
        results = lax.dynamic_update_index_in_dim(
            results, jnp.where(active, output_rows, previous), micro_index, 0
        )
        if step_number + 1 < tick_total:
            received = from_behind(output_rows, "section", 1)
    return results[None]


def solution(mesh):
    placed = (
        P(None, "ep", "tp"),
        P("section", None),
        P("section", "ep", None, "tp"),
        P("section", "ep", None, "tp"),
        P("section", "ep", "tp", None),
        P("section", None, "ep", None),
        P("section", None, "ep", None),
    )
    return jax.shard_map(
        shards,
        mesh=mesh,
        in_specs=placed,
        out_specs=P("section", None, "ep", "tp"),
        check_vma=False,
    )
```

profile of v0, /device:TPU:1, one launch (start us, length us, event | category | flops | bytes accessed | tf_op | source)
XLA Modules:
  0.0 744.3 jit_solution(17308153850093441637)
XLA Ops:
  7.6 1.2 reduce-window.20
  9.8 1.0 fusion.62
  10.8 9.3 %psum.21 = f32[64]{0:T(128)S(1)} all-reduce(f32[64]{0:T(128)S(1)} %fusion.62), channel_id=1, replica_groups=mesh['section'=2,'tp'=4,'ep'=64] {'tp'}, use_global_device_ids=true, to_apply=%region_5.6 | all-reduce | flops 64 | bytes 512 | tf_op jit(solution)/shard_map/psum | solution.py:49
  20.8 1.2 convolution_convert_fusion.5
  22.3 67.6 %all_to_all.45 = bf16[64,9,512]{2,1,0:T(8,128)(2,1)} all-to-all(bf16[64,9,512]{2,1,0:T(8,128)(2,1)S(1)} %reshape.205), channel_id=1, replica_groups=mesh['section'=2,'tp'=4,'ep'=64] {'ep'}, dimensions={0} | all-to-all | bytes 1179648 | tf_op jit(solution)/shard_map/all_to_all | solution.py:54
  89.9 51.7 %all-gather.4.cloned.1.call-done = bf16[64,9,2048]{2,1,0:T(8,128)(2,1)} async-done(((bf16[64,9,512]{2,1,0:T(8,128)(2,1)}), bf16[64,9,2048]{2,1,0:T(8,128)(2,1)}) %all-gather.4.cloned.1.call-update) | async-done | bytes 2359312 | tf_op jit(solution)/shard_map/all_gather | solution.py:61
  141.7 3.4 reshape.206
  145.1 2.8 fusion.19
  147.9 5.4 convolution_convert_fusion.2
  153.2 1.8 copy.69
  155.1 31.1 %all_to_all.46 = bf16[576,4,512]{2,0,1:T(8,128)(2,1)S(1)} all-to-all(bf16[576,4,512]{2,0,1:T(8,128)(2,1)S(1)} %bitcast.188), channel_id=1, replica_groups=mesh['section'=2,'tp'=4,'ep'=64] {'tp'}, dimensions={1} | all-to-all | bytes 4718592 | tf_op jit(solution)/shard_map/all_to_all | solution.py:70
  186.2 1.3 reduce_sum.99
  187.6 2.2 reshape.208
  189.8 15.4 %all-to-all-start.2 = ((bf16[64,9,512]{2,1,0:T(8,128)(2,1)}), bf16[64,9,512]{2,1,0:T(8,128)(2,1)S(1)}, u32[]{:S(2)}, u32[]{:S(2)}) async-start(bf16[64,9,512]{2,1,0:T(8,128)(2,1)} %reshape.208), calls=%async_computation.2 | async-start | bytes 2097152 | tf_op jit(solution)/shard_map/all_to_all | solution.py:78
  206.2 1.2 reduce-window.24
  207.9 48.0 %all-to-all-done.2 = bf16[64,9,512]{2,1,0:T(8,128)(2,1)S(1)} async-done(((bf16[64,9,512]{2,1,0:T(8,128)(2,1)}), bf16[64,9,512]{2,1,0:T(8,128)(2,1)S(1)}, u32[]{:S(2)}, u32[]{:S(2)}) %all-to-all-start.2) | async-done | bytes 589856 | tf_op jit(solution)/shard_map/all_to_all | solution.py:78
  256.2 2.0 gather_fusion
  258.9 1.3 collective-permute-start
  260.7 5.7 collective-permute-done
  266.5 6.9 psum.22
  274.0 55.0 %all_to_all.47 = bf16[64,9,512]{2,1,0:T(8,128)(2,1)} all-to-all(bf16[64,9,512]{2,1,0:T(8,128)(2,1)S(1)} %reshape.212), channel_id=1, replica_groups=mesh['section'=2,'tp'=4,'ep'=64] {'ep'}, dimensions={0} | all-to-all | bytes 1179648 | tf_op jit(solution)/shard_map/all_to_all | solution.py:54
  329.0 51.8 %all-gather.6.cloned.1.call-done = bf16[64,9,2048]{2,1,0:T(8,128)(2,1)} async-done(((bf16[64,9,512]{2,1,0:T(8,128)(2,1)}), bf16[64,9,2048]{2,1,0:T(8,128)(2,1)}) %all-gather.6.cloned.1.call-update) | async-done | bytes 2359312 | tf_op jit(solution)/shard_map/all_gather | solution.py:61
  380.8 3.4 reshape.213
  384.2 2.8 fusion.17
  387.0 5.4 convolution_convert_fusion.1
  392.4 1.8 copy.68
  394.2 31.1 %all_to_all.48 = bf16[576,4,512]{2,0,1:T(8,128)(2,1)S(1)} all-to-all(bf16[576,4,512]{2,0,1:T(8,128)(2,1)S(1)} %bitcast.189), channel_id=1, replica_groups=mesh['section'=2,'tp'=4,'ep'=64] {'tp'}, dimensions={1} | all-to-all | bytes 4718592 | tf_op jit(solution)/shard_map/all_to_all | solution.py:70
  425.3 1.3 reduce_sum.103
  426.7 2.2 reshape.215
  428.9 15.4 %all-to-all-start.5 = ((bf16[64,9,512]{2,1,0:T(8,128)(2,1)}), bf16[64,9,512]{2,1,0:T(8,128)(2,1)S(1)}, u32[]{:S(2)}, u32[]{:S(2)}) async-start(bf16[64,9,512]{2,1,0:T(8,128)(2,1)} %reshape.215), calls=%async_computation.5 | async-start | bytes 2097152 | tf_op jit(solution)/shard_map/all_to_all | solution.py:78
  445.3 1.2 reduce-window.26
  448.7 46.3 %all-to-all-done.5 = bf16[64,9,512]{2,1,0:T(8,128)(2,1)S(1)} async-done(((bf16[64,9,512]{2,1,0:T(8,128)(2,1)}), bf16[64,9,512]{2,1,0:T(8,128)(2,1)S(1)}, u32[]{:S(2)}, u32[]{:S(2)}) %all-to-all-start.5) | async-done | bytes 589856 | tf_op jit(solution)/shard_map/all_to_all | solution.py:78
  495.4 2.0 gather_fusion.1
  498.1 1.3 collective-permute-start.1
  499.9 5.7 collective-permute-done.1
  505.7 6.9 psum.23
  513.2 56.2 %all_to_all.49 = bf16[64,9,512]{2,1,0:T(8,128)(2,1)} all-to-all(bf16[64,9,512]{2,1,0:T(8,128)(2,1)S(1)} %reshape.219), channel_id=1, replica_groups=mesh['section'=2,'tp'=4,'ep'=64] {'ep'}, dimensions={0} | all-to-all | bytes 1179648 | tf_op jit(solution)/shard_map/all_to_all | solution.py:54
  569.4 50.6 %all-gather.8.cloned.1.call-done = bf16[64,9,2048]{2,1,0:T(8,128)(2,1)} async-done(((bf16[64,9,512]{2,1,0:T(8,128)(2,1)}), bf16[64,9,2048]{2,1,0:T(8,128)(2,1)}) %all-gather.8.cloned.1.call-update) | async-done | bytes 2359312 | tf_op jit(solution)/shard_map/all_gather | solution.py:61
  620.0 3.4 reshape.220
  623.4 2.8 fusion.15
  626.2 5.4 convolution_convert_fusion
  631.6 1.8 copy.67
  633.4 31.1 %all_to_all.50 = bf16[576,4,512]{2,0,1:T(8,128)(2,1)S(1)} all-to-all(bf16[576,4,512]{2,0,1:T(8,128)(2,1)S(1)} %bitcast.190), channel_id=1, replica_groups=mesh['section'=2,'tp'=4,'ep'=64] {'tp'}, dimensions={1} | all-to-all | bytes 4718592 | tf_op jit(solution)/shard_map/all_to_all | solution.py:70
  664.5 1.3 reduce_sum.107
  665.9 2.2 reshape.222
  668.1 15.4 %all-to-all-start.8 = ((bf16[64,9,512]{2,1,0:T(8,128)(2,1)}), bf16[64,9,512]{2,1,0:T(8,128)(2,1)S(1)}, u32[]{:S(2)}, u32[]{:S(2)}) async-start(bf16[64,9,512]{2,1,0:T(8,128)(2,1)} %reshape.222), calls=%async_computation.8 | async-start | bytes 2097152 | tf_op jit(solution)/shard_map/all_to_all | solution.py:78
  684.2 50.0 %all-to-all-done.8 = bf16[64,9,512]{2,1,0:T(8,128)(2,1)S(1)} async-done(((bf16[64,9,512]{2,1,0:T(8,128)(2,1)}), bf16[64,9,512]{2,1,0:T(8,128)(2,1)S(1)}, u32[]{:S(2)}, u32[]{:S(2)}) %all-to-all-start.8) | async-done | bytes 589856 | tf_op jit(solution)/shard_map/all_to_all | solution.py:78
  734.5 2.0 gather_fusion.2
  (105 shorter events, 14.4 us)
Async XLA Ops:
  6.5 141.4 %copy-start = (bf16[1,1,256,2048]{3,2,1,0:T(8,128)(2,1)S(1)}, bf16[1,1,256,2048]{3,2,1,0:T(8,128)(2,1)}, u32[]{:S(2)}) copy-start(bf16[1,1,256,2048]{3,2,1,0:T(8,128)(2,1)} %param.13) | copy-start | bytes 3145732
  6.5 135.1 %all-gather.4.cloned.1.call-start = ((), (), s32[]{:S(2)}) async-start(), calls=%async_computation.9 | async-start | bytes 5242880 | tf_op jit(solution)/shard_map/all_gather | solution.py:61
  187.5 17.9 %copy-start.12 = (f32[1,2,64,8]{2,3,1,0:T(8,128)S(1)}, f32[1,2,64,8]{2,3,1,0:T(8,128)}, u32[]{:S(2)}) copy-start(f32[1,2,64,8]{2,3,1,0:T(8,128)} %param.15) | copy-start | bytes 12292
  189.8 66.2 %all-to-all-start.2 = ((bf16[64,9,512]{2,1,0:T(8,128)(2,1)}), bf16[64,9,512]{2,1,0:T(8,128)(2,1)S(1)}, u32[]{:S(2)}, u32[]{:S(2)}) async-start(bf16[64,9,512]{2,1,0:T(8,128)(2,1)} %reshape.208), calls=%async_computation.2 | async-start | bytes 2097152 | tf_op jit(solution)/shard_map/all_to_all | solution.py:78
  205.1 175.7 %all-gather.6.cloned.1.call-start = ((), (), s32[]{:S(2)}) async-start(), calls=%async_computation.10 | async-start | bytes 5242880 | tf_op jit(solution)/shard_map/all_gather | solution.py:61
  256.2 2.6 copy-start.1
  258.9 7.5 %collective-permute-start = (bf16[64,512]{1,0:T(8,128)(2,1)S(1)}, bf16[64,512]{1,0:T(8,128)(2,1)S(1)}, u32[]{:S(2)}, u32[]{:S(2)}) collective-permute-start(bf16[64,512]{1,0:T(8,128)(2,1)S(1)} %get-tuple-element.17), channel_id=1, source_target_pairs={{0,256},{1,257},{2,258},{3,259},{4,260},{5,261},{6,262},{7,263},{8... | collective-permute-start | bytes 196616 | tf_op jit(solution)/shard_map/ppermute | solution.py:12
  266.5 62.5 %copy-start.5 = (bf16[64,512]{1,0:T(8,128)(2,1)}, bf16[64,512]{1,0:T(8,128)(2,1)S(1)}, u32[]{:S(2)}) copy-start(bf16[64,512]{1,0:T(8,128)(2,1)S(1)} %get-tuple-element.15) | copy-start | bytes 196612
  426.7 17.9 %copy-start.14 = (f32[64,8,1]{0,1,2:T(8,128)S(1)}, f32[64,8,1]{0,1,2:T(8,128)}, u32[]{:S(2)}) copy-start(f32[64,8,1]{0,1,2:T(8,128)} %get-tuple-element.25) | copy-start | bytes 6148
  428.9 66.2 %all-to-all-start.5 = ((bf16[64,9,512]{2,1,0:T(8,128)(2,1)}), bf16[64,9,512]{2,1,0:T(8,128)(2,1)S(1)}, u32[]{:S(2)}, u32[]{:S(2)}) async-start(bf16[64,9,512]{2,1,0:T(8,128)(2,1)} %reshape.215), calls=%async_computation.5 | async-start | bytes 2097152 | tf_op jit(solution)/shard_map/all_to_all | solution.py:78
  444.2 175.7 %all-gather.8.cloned.1.call-start = ((), (), s32[]{:S(2)}) async-start(), calls=%async_computation.11 | async-start | bytes 5242880 | tf_op jit(solution)/shard_map/all_gather | solution.py:61
  446.9 1.9 copy-start.10
  495.3 2.0 copy-start.9
  495.3 2.0 copy-start.15
  495.3 2.7 copy-start.6
  495.3 2.7 copy-start.7
  495.4 4.0 copy-start.8
  495.4 10.2 %copy-start.2 = (bf16[2,64,512]{2,1,0:T(8,128)(2,1)S(1)}, bf16[2,64,512]{2,1,0:T(8,128)(2,1)}, u32[]{:S(2)}) copy-start(bf16[2,64,512]{2,1,0:T(8,128)(2,1)} %param.9) | copy-start | bytes 393220
  498.1 7.5 %collective-permute-start.1 = (bf16[64,512]{1,0:T(8,128)(2,1)S(1)}, bf16[64,512]{1,0:T(8,128)(2,1)S(1)}, u32[]{:S(2)}, u32[]{:S(2)}) collective-permute-start(bf16[64,512]{1,0:T(8,128)(2,1)S(1)} %get-tuple-element.11), channel_id=1, source_target_pairs={{0,256},{1,257},{2,258},{3,259},{4,260},{5,261},{6,262},{7,263},{8... | collective-permute-start | bytes 196616 | tf_op jit(solution)/shard_map/ppermute | solution.py:12
  505.7 63.8 %copy-start.3 = (bf16[64,512]{1,0:T(8,128)(2,1)}, bf16[64,512]{1,0:T(8,128)(2,1)S(1)}, u32[]{:S(2)}) copy-start(bf16[64,512]{1,0:T(8,128)(2,1)S(1)} %get-tuple-element.9) | copy-start | bytes 196612
  665.9 17.6 %copy-start.13 = (f32[64,8,1]{0,1,2:T(8,128)S(1)}, f32[64,8,1]{0,1,2:T(8,128)}, u32[]{:S(2)}) copy-start(f32[64,8,1]{0,1,2:T(8,128)} %get-tuple-element.23) | copy-start | bytes 6148
  665.9 17.7 %copy-start.11 = (s32[512]{0:T(512)S(1)}, s32[512]{0:T(512)}, u32[]{:S(2)}) copy-start(s32[512]{0:T(512)} %copy-done.10) | copy-start | bytes 6148
  668.1 66.2 %all-to-all-start.8 = ((bf16[64,9,512]{2,1,0:T(8,128)(2,1)}), bf16[64,9,512]{2,1,0:T(8,128)(2,1)S(1)}, u32[]{:S(2)}, u32[]{:S(2)}) async-start(bf16[64,9,512]{2,1,0:T(8,128)(2,1)} %reshape.222), calls=%async_computation.8 | async-start | bytes 2097152 | tf_op jit(solution)/shard_map/all_to_all | solution.py:78
  734.5 2.6 copy-start.4
Sparse Core Ops, SparseCore 0:
  90.0 51.5 all-gather.3
  329.1 51.6 all-gather.5
  569.5 50.4 all-gather.7
where the time goes:
time: 749 us; the launch traced here: 744 us
  waiting for transfers between devices  310 us (41%)
  blocking collectives  295 us (39%)
  starting transfers between devices  48.8 us (7%)
  local copies, waits for them, and re-layouts  35.7 us (5%)
  matrix products  28.5 us (4%)
  between operations  13.7 us (2%)
  other arithmetic  12.7 us (2%)
    all_to_all x3, blocking collectives, shards(): lax.all_to_all(buffer.reshape(expert_count, capacity, quarter), 'ep', spl...  179 us
    all_gather x3, waiting for transfers between devices, shards(): shard_part = lax.all_gather(arrived, 'tp', axis=2, tiled=True)  154 us
    all_to_all x3, waiting for transfers between devices, shards(): lax.all_to_all(expert_out.reshape(expert_count, capacity, quarter), 'ep',...  144 us
    all_to_all x3, blocking collectives, shards(): lax.all_to_all(partial_value.reshape(slot_total, tensor_count, quarter),...  93.4 us
    all_to_all x3, starting transfers between devices, shards(): lax.all_to_all(expert_out.reshape(expert_count, capacity, quarter), 'ep',...  46.1 us
    psum x3, blocking collectives, shards(): square_sum = lax.psum(jnp.sum(values * values, axis=1), 'tp')  23.1 us
    dot_general x3, matrix products, shards(): jnp.dot(hidden, weight_down, preferred_element_type=jnp.float32)  16.1 us
  transfers between devices with their start and end apart: 8, of which 8 were waited for; matrix products, arithmetic and copies ran while one was open for 1% of the time, Pallas kernels for 0%

commit v1 on v0

v1 whole, which is shorter than its diff:
```python
import jax
import jax.numpy as jnp
from jax import lax
from jax.experimental import pallas as pl
from jax.experimental.pallas import tpu as pltpu
from jax.sharding import PartitionSpec as P

EPSILON = 1e-06
NZ, NY, NX = 16, 4, 4
TOK, TOPK, CAP = 64, 8, 9
D, Q, FFQ = 2048, 512, 256
ROWS = NZ * CAP
MESH = pl.DeviceIdType.MESH
BF, F32 = jnp.bfloat16, jnp.float32


def remote(src, dst, send, recv, device):
    return pltpu.make_async_remote_copy(
        src_ref=src,
        dst_ref=dst,
        send_sem=send,
        recv_sem=recv,
        device_id=device,
        device_id_type=MESH,
    )


def kernel(
    tokens,
    gain_in,
    meta_in,
    gate_in,
    up_in,
    down_in,
    out,
    gate,
    up,
    down,
    gains,
    blocks,
    meta,
    chosen,
    rows,
    parts,
    half,
    half_out,
    half_in,
    done,
    back,
    pick,
    mix,
    ring_out,
    ring_in,
    results,
    sibling_result,
    local_sem,
    pair_send,
    pair_recv,
    zg_send,
    zg_recv,
    zm_send,
    zm_recv,
    yg_send,
    yg_recv,
    yr_send,
    yr_recv,
    xg_send,
    xg_recv,
    xr_send,
    xr_recv,
    zr_send,
    zr_recv,
):
    core = lax.axis_index("section")
    x = lax.axis_index("tp")
    ep = lax.axis_index("ep")
    z, y = ep // NY, ep % NY
    sibling = (1 - core, x, ep)
    z_up = (core, x, ((z + 1) % NZ) * NY + y)
    z_down = (core, x, ((z + NZ - 1) % NZ) * NY + y)

    def at_y(step):
        return (core, x, z * NY + (y + step + NY) % NY)

    x_one = x + 1 - 2 * (x % 2)
    x_three = 3 - x
    x_two = (x + 2) % 4
    quarter = (x, x_one, x_two, x_three)

    def at_x(which):
        return (core, which, ep)

    barrier = pltpu.get_barrier_semaphore()
    friends = [sibling, z_up, z_down, at_y(1), at_y(2), at_y(3), at_x(x_one), at_x(x_three)]
    for friend in friends:
        pl.semaphore_signal(barrier, inc=1, device_id=friend, device_id_type=MESH)
    pl.semaphore_wait(barrier, len(friends))

    def pair_copies():
        sources = (
            (meta_in.at[1 - core], meta.at[0, core]),
            (gain_in, gains.at[core]),
            (gate_in, gate.at[core]),
            (up_in, up.at[core]),
            (down_in, down.at[core]),
        )
        return [
            remote(src, dst, pair_send.at[n], pair_recv.at[n], sibling)
            for n, (src, dst) in enumerate(sources)
        ]

    def own_copies():
        sources = (
            (meta_in.at[core], meta.at[0, core]),
            (gain_in, gains.at[core]),
            (gate_in, gate.at[core]),
            (up_in, up.at[core]),
            (down_in, down.at[core]),
        )
        return [
            pltpu.make_async_copy(src, dst, local_sem.at[n]) for n, (src, dst) in enumerate(sources)
        ]

    pair, own = pair_copies(), own_copies()
    for copy in pair[:1] + own[:1]:
        copy.start()

    def gather_down(layer, step, src):
        return remote(
            blocks.at[layer, src],
            blocks.at[layer, 2 * step - 1],
            zg_send.at[layer, 0, step - 1],
            zg_recv.at[layer, 0, step - 1],
            z_down,
        )

    def gather_up(layer, step, src):
        return remote(
            blocks.at[layer, src],
            blocks.at[layer, 2 * step],
            zg_send.at[layer, 1, step - 1],
            zg_recv.at[layer, 1, step - 1],
            z_up,
        )

    def meta_down(step, src):
        return remote(
            meta.at[src], meta.at[2 * step - 1], zm_send.at[0, step - 1], zm_recv.at[0, step - 1], z_down
        )

    def meta_up(step, src):
        return remote(
            meta.at[src], meta.at[2 * step], zm_send.at[1, step - 1], zm_recv.at[1, step - 1], z_up
        )

    def y_go(layer, n):
        return remote(
            chosen.at[layer, n],
            rows.at[layer, n, 0],
            yg_send.at[layer, n],
            yg_recv.at[layer, n],
            at_y(n),
        )

    def y_back(layer, n):
        return remote(
            done.at[layer, n],
            back.at[layer, n],
            yr_send.at[layer, n],
            yr_recv.at[layer, n],
            at_y(-n),
        )

    def swap(n):
        odd = n % 2
        first, second = 1 + 2 * odd, 3 - 2 * odd
        first_at = x_one + odd * (x_three - x_one)
        second_at = x_three + odd * (x_one - x_three)
        return first, second, at_x(first_at), at_x(second_at)

    def x_gather(layer, n):
        first, second, first_at, second_at = swap(n)
        sems = lambda k: (xg_send.at[layer, n, k], xg_recv.at[layer, n, k])
        own_rows = rows.at[layer, n, 0]
        return (
            remote(own_rows, rows.at[layer, n, first], *sems(0), first_at),
            remote(own_rows, rows.at[layer, n, second], *sems(1), second_at),
            remote(rows.at[layer, n, first], rows.at[layer, n, 2], *sems(2), second_at),
        )

    def x_reduce(layer, n):
        first, second, first_at, second_at = swap(n)
        sems = lambda k: (xr_send.at[layer, n, k], xr_recv.at[layer, n, k])
        return (
            remote(parts.at[layer, n, 2], half.at[layer, n, 1], *sems(0), first_at),
            remote(parts.at[layer, n, first], half.at[layer, n, 0], *sems(1), first_at),
            remote(half_out.at[layer, n], half_in.at[layer, n], *sems(2), second_at),
        )

    def reduce_up(layer, step):
        return remote(
            ring_out.at[layer, 0, step - 1],
            ring_in.at[layer, 0, step - 1],
            zr_send.at[layer, 0, step - 1],
            zr_recv.at[layer, 0, step - 1],
            z_up,
        )

    def reduce_down(layer, step):
        return remote(
            ring_out.at[layer, 1, step - 1],
            ring_in.at[layer, 1, step - 1],
            zr_send.at[layer, 1, step - 1],
            zr_recv.at[layer, 1, step - 1],
            z_down,
        )

    def build_selection(layer):
        lane = lax.broadcasted_iota(jnp.int32, (TOPK, 128), 1)
        low = lane < TOK
        a = lax.broadcasted_iota(jnp.int32, (128, 128), 0)
        b = lax.broadcasted_iota(jnp.int32, (128, 128), 1)
        before = jnp.where((a < b) & ((a < TOK) == (b < TOK)), 1.0, 0.0).astype(BF)
        row_number = lax.broadcasted_iota(jnp.int32, (ROWS, 128), 0).astype(F32)
        high_one = jnp.where(lax.broadcasted_iota(jnp.int32, (1, 128), 1) < TOK, 0.0, 1.0)
        experts = [(z * NY + (y + n) % NY).astype(F32) for n in range(NY)]

        def pair_of_blocks(q, carry):
            named = jnp.where(low, meta[2 * q, layer, 0:TOPK], meta[2 * q + 1, layer, 0:TOPK])
            weight = jnp.where(
                low, meta[2 * q, layer, TOPK : 2 * TOPK], meta[2 * q + 1, layer, TOPK : 2 * TOPK]
            )
            base = (2 * q).astype(F32) + high_one
            lanes = pl.ds(pl.multiple_of(q * 128, 128), 128)
            for n in range(NY):
                same = jnp.where(named == experts[n], 1.0, 0.0)
                count = jnp.dot(same.astype(BF), before, preferred_element_type=F32)
                position = jnp.sum(count, axis=0, keepdims=True)
                hits = jnp.sum(same, axis=0, keepdims=True)
                share = jnp.sum(same * weight, axis=0, keepdims=True)
                slot = jnp.where(hits > 0.5, position + CAP * base, -1.0)
                hit = row_number == slot
                pick[n, :, lanes] = jnp.where(hit, 1.0, 0.0).astype(BF)
                mix[q, n * ROWS : (n + 1) * ROWS, :] = jnp.where(hit, share, 0.0).astype(BF)
            return carry

        lax.fori_loop(0, NZ // 2, pair_of_blocks, 0)

    def expert(layer, n):
        first, second, _, _ = swap(n)
        total = jnp.zeros((ROWS, 1), F32)
        for s in range(4):
            value = rows[layer, n, s].astype(F32)
            total = total + jnp.sum(value * value, axis=1, keepdims=True)
        scale = lax.rsqrt(total / D + EPSILON)
        gate_act = jnp.zeros((ROWS, FFQ), F32)
        up_act = jnp.zeros((ROWS, FFQ), F32)
        for s in range(4):
            span = pl.ds(pl.multiple_of(quarter[s] * Q, Q), Q)
            value = rows[layer, n, s].astype(F32)
            normed = (value * scale * gains[layer, 0:1, span]).astype(BF)
            gate_act += jnp.dot(normed, gate[layer, span, :], preferred_element_type=F32)
            up_act += jnp.dot(normed, up[layer, span, :], preferred_element_type=F32)
        hidden = (gate_act / (1.0 + jnp.exp(-gate_act)) * up_act).astype(BF)
        sends = x_reduce(layer, n)
        for s in (2, 1, 3, 0):
            span = pl.ds(pl.multiple_of(quarter[s] * Q, Q), Q)
            parts[layer, n, s] = jnp.dot(
                hidden, down[layer, :, span], preferred_element_type=F32
            ).astype(BF)
            if s == 2:
                sends[0].start()
            if s == 3:
                sends[1].start()

    def mixed(layer, q):
        returned = back[layer].reshape(NY * ROWS, Q)
        return lax.dot_general(
            mix[q], returned, (((0,), (0,)), ((), ())), preferred_element_type=F32
        )

    def one_layer(layer, carry):
        gather_down(layer, 1, 0).start()
        gather_up(layer, 1, 0).start()

        @pl.when(layer == 0)
        def _():
            for copy in pair[1:] + own[1:]:
                copy.start()
            own[0].wait()
            pair[0].wait()
            meta_down(1, 0).start()
            meta_up(1, 0).start()

        def gather_step(step, c):
            gather_down(layer, step - 1, 0).wait_recv()
            gather_down(layer, step, 2 * step - 3).start()
            gather_up(layer, step - 1, 0).wait_recv()

            @pl.when(step < 8)
            def _():
                gather_up(layer, step, 2 * step - 2).start()

            @pl.when(layer == 0)
            def _():
                meta_down(step - 1, 0).wait_recv()
                meta_down(step, 2 * step - 3).start()
                meta_up(step - 1, 0).wait_recv()

                @pl.when(step < 8)
                def _():
                    meta_up(step, 2 * step - 2).start()

            return c

        lax.fori_loop(2, 9, gather_step, 0)
        gather_down(layer, 8, 0).wait_recv()

        @pl.when(layer == 0)
        def _():
            meta_down(8, 0).wait_recv()

        build_selection(layer)
        everything = blocks[layer].reshape(NZ * TOK, Q)
        for n in (1, 2, 3, 0):
            value = jnp.dot(pick[n], everything, preferred_element_type=F32).astype(BF)
            if n == 0:
                rows[layer, 0, 0] = value
            else:
                chosen[layer, n] = value
                y_go(layer, n).start()

        @pl.when(layer == 0)
        def _():
            for copy in pair[1:] + own[1:]:
                copy.wait()

        def tick(t, c):
            @pl.when(t < 4)
            def _():
                @pl.when(t > 0)
                def _():
                    y_go(layer, t).wait_recv()

                own_first, own_second, _ = x_gather(layer, t)
                own_first.start()
                own_second.start()

            @pl.when((t >= 1) & (t < 5))
            def _():
                got_first, _, forward = x_gather(layer, t - 1)
                got_first.wait_recv()
                forward.start()

            @pl.when((t >= 3) & (t < 7))
            def _():
                n = t - 3
                far, near, onward = x_reduce(layer, n)
                far.wait_recv()
                _, second, _, _ = swap(n)
                half_out[layer, n] = (
                    parts[layer, n, second].astype(F32) + half[layer, n, 1].astype(F32)
                ).astype(BF)
                onward.start()

            @pl.when((t >= 2) & (t < 6))
            def _():
                _, got_second, forward = x_gather(layer, t - 2)
                got_second.wait_recv()
                forward.wait_recv()
                expert(layer, t - 2)

            @pl.when(t >= 4)
            def _():
                n = t - 4
                far, near, onward = x_reduce(layer, n)
                near.wait_recv()
                onward.wait_recv()
                value = (
                    parts[layer, n, 0].astype(F32)
                    + half[layer, n, 0].astype(F32)
                    + half_in[layer, n].astype(F32)
                ).astype(BF)

                @pl.when(n == 0)
                def _():
                    back[layer, 0] = value

                @pl.when(n > 0)
                def _():
                    done[layer, n] = value
                    y_back(layer, n).start()

            return c

        lax.fori_loop(0, 8, tick, 0)
        for n in range(1, 4):
            y_back(layer, n).wait_recv()

        value = mixed(layer, NZ // 2 - 1)
        ring_out[layer, 0, 0] = value[TOK:].astype(BF)
        reduce_up(layer, 1).start()
        ring_out[layer, 1, 0] = value[:TOK].astype(BF)
        reduce_down(layer, 1).start()

        def reduce_step(step, c):
            value = mixed(layer, NZ // 2 - step)
            reduce_up(layer, step - 1).wait_recv()
            ring_out[layer, 0, step - 1] = (
                value[TOK:] + ring_in[layer, 0, step - 2].astype(F32)
            ).astype(BF)
            reduce_up(layer, step).start()
            reduce_down(layer, step - 1).wait_recv()
            ring_out[layer, 1, step - 1] = (
                value[:TOK] + ring_in[layer, 1, step - 2].astype(F32)
            ).astype(BF)
            reduce_down(layer, step).start()
            return c

        lax.fori_loop(2, 8, reduce_step, 0)
        value = mixed(layer, 0)
        reduce_up(layer, 7).wait_recv()
        ring_out[layer, 0, 7] = (value[TOK:] + ring_in[layer, 0, 6].astype(F32)).astype(BF)
        reduce_up(layer, 8).start()
        reduce_down(layer, 7).wait_recv()
        mine = value[:TOK] + blocks[layer, 0].astype(F32) + ring_in[layer, 1, 6].astype(F32)
        reduce_up(layer, 8).wait_recv()
        final = (mine + ring_in[layer, 0, 7].astype(F32)).astype(BF)
        results[layer] = final

        @pl.when(layer == 0)
        def _():
            blocks[1, 0] = final

        return carry

    blocks[0, 0] = tokens[core]
    lax.fori_loop(0, 2, one_layer, 0)
    last = remote(results.at[1 - core], sibling_result, pair_send.at[5], pair_recv.at[5], sibling)
    last.start()
    out[core] = results[core]

    def drain(layer, carry):
        def ring(step, c):
            gather_down(layer, step, 0).wait_send()
            reduce_up(layer, step).wait_send()

            @pl.when(step < 8)
            def _():
                gather_up(layer, step, 0).wait_send()
                reduce_down(layer, step).wait_send()

            @pl.when(layer == 0)
            def _():
                meta_down(step, 0).wait_send()

                @pl.when(step < 8)
                def _():
                    meta_up(step, 0).wait_send()

            return c

        lax.fori_loop(1, 9, ring, 0)

        def chunk(n, c):
            for copy in x_gather(layer, n) + x_reduce(layer, n):
                copy.wait_send()

            @pl.when(n > 0)
            def _():
                y_go(layer, n).wait_send()
                y_back(layer, n).wait_send()

            return c

        lax.fori_loop(0, 4, chunk, 0)
        return carry

    lax.fori_loop(0, 2, drain, 0)
    last.wait()
    out[1 - core] = sibling_result[...]


def shards(tokens, norm_gain, expert_gate, expert_up, expert_down, routes, route_weights):
    named = jnp.swapaxes(routes[0], 1, 2).astype(F32)
    weight = jnp.swapaxes(route_weights[0], 1, 2)
    meta = jnp.concatenate([named, weight], axis=1)
    meta = jnp.concatenate([meta, meta], axis=2)
    gain = jnp.broadcast_to(norm_gain, (8, D))
    vmem = pl.BlockSpec(memory_space=pltpu.VMEM)
    anywhere = pl.BlockSpec(memory_space=pl.ANY)
    dma = pltpu.SemaphoreType.DMA
    out = pl.pallas_call(
        kernel,
        out_shape=jax.ShapeDtypeStruct((2, TOK, Q), BF),
        in_specs=[vmem, vmem, vmem, anywhere, anywhere, anywhere],
        out_specs=vmem,
        scratch_shapes=[
            pltpu.VMEM((2, D, FFQ), BF),
            pltpu.VMEM((2, D, FFQ), BF),
            pltpu.VMEM((2, FFQ, D), BF),
            pltpu.VMEM((2, 8, D), F32),
            pltpu.VMEM((2, NZ, TOK, Q), BF),
            pltpu.VMEM((NZ, 2, 2 * TOPK, 128), F32),
            pltpu.VMEM((2, NY, ROWS, Q), BF),
            pltpu.VMEM((2, NY, 4, ROWS, Q), BF),
            pltpu.VMEM((2, NY, 4, ROWS, Q), BF),
            pltpu.VMEM((2, NY, 2, ROWS, Q), BF),
            pltpu.VMEM((2, NY, ROWS, Q), BF),
            pltpu.VMEM((2, NY, ROWS, Q), BF),
            pltpu.VMEM((2, NY, ROWS, Q), BF),
            pltpu.VMEM((2, NY, ROWS, Q), BF),
            pltpu.VMEM((NY, ROWS, NZ * TOK), BF),
            pltpu.VMEM((NZ // 2, NY * ROWS, 128), BF),
            pltpu.VMEM((2, 2, 8, TOK, Q), BF),
            pltpu.VMEM((2, 2, 8, TOK, Q), BF),
            pltpu.VMEM((2, TOK, Q), BF),
            pltpu.VMEM((TOK, Q), BF),
            dma((5,)),
            dma((6,)),
            dma((6,)),
            dma((2, 2, 8)),
            dma((2, 2, 8)),
            dma((2, 8)),
            dma((2, 8)),
            dma((2, 4)),
            dma((2, 4)),
            dma((2, 4)),
            dma((2, 4)),
            dma((2, 4, 3)),
            dma((2, 4, 3)),
            dma((2, 4, 3)),
            dma((2, 4, 3)),
            dma((2, 2, 8)),
            dma((2, 2, 8)),
        ],
        compiler_params=pltpu.CompilerParams(
            collective_id=0, has_side_effects=True, vmem_limit_bytes=56 * 1024 * 1024
        ),
        cost_estimate=pl.CostEstimate(
            flops=2 * 2 * 576 * D * 768, bytes_accessed=8 * 1024 * 1024, transcendentals=0
        ),
    )(tokens, gain, meta, expert_gate[0, 0], expert_up[0, 0], expert_down[0, 0])
    return out[None]


def solution(mesh):
    placed = (
        P(None, "ep", "tp"),
        P("section", None),
        P("section", "ep", None, "tp"),
        P("section", "ep", None, "tp"),
        P("section", "ep", "tp", None),
        P("section", None, "ep", None),
        P("section", None, "ep", None),
    )
    return jax.shard_map(
        shards,
        mesh=mesh,
        in_specs=placed,
        out_specs=P("section", None, "ep", "tp"),
        check_vma=False,
    )
```

time: 749 us -> 232 us (0.31)
  waiting for transfers between devices: 310 us -> 0 us
  blocking collectives: 295 us -> 0 us
  Pallas kernels: 0 us -> 228 us
  starting transfers between devices: 48.8 us -> 0 us
  local copies, waits for them, and re-layouts: 35.7 us -> 3.61 us
  matrix products: 28.5 us -> 0 us
  between operations: 13.7 us -> 0.01 us
  other arithmetic: 12.7 us -> 0.68 us
    all_to_all x6 -> x0, blocking collectives: 272 us -> none  [the longest x3 179 us: shards(): lax.all_to_all(buffer.reshape(expert_count, capacity, quarter), 'ep', spl...]
    pallas_call x0 -> x1, Pallas kernels: none -> 228 us  [shards(): pl.pallas_call(kernel, out_shape=jax.ShapeDtypeStruct((2, TOK, Q), BF), i...]
    all_gather x3 -> x0, waiting for transfers between devices: 154 us -> none  [shards(): shard_part = lax.all_gather(arrived, 'tp', axis=2, tiled=True)]
    all_to_all x3 -> x0, waiting for transfers between devices: 144 us -> none  [shards(): lax.all_to_all(expert_out.reshape(expert_count, capacity, quarter), 'ep',...]
    all_to_all x3 -> x0, starting transfers between devices: 46.1 us -> none  [shards(): lax.all_to_all(expert_out.reshape(expert_count, capacity, quarter), 'ep',...]
    dot_general x12 -> x0, matrix products: 28.5 us -> none  [the longest x3 16.1 us: shards(): jnp.dot(hidden, weight_down, preferred_element_type=jnp.float32)]
    reshape x15 -> x0, local copies, waits for them, and re-layouts: 23.7 us -> none  [the longest x3 10.1 us: shards(): rows_part = shard_part.reshape(slot_total, feature_count)]
    psum x3 -> x0, blocking collectives: 23.1 us -> none  [shards(): square_sum = lax.psum(jnp.sum(values * values, axis=1), 'tp')]
  transfers between devices with their start and end apart: 8 -> 0, of which waited for: 8 -> 0; matrix products, arithmetic and copies ran while one was open for 1% -> 0% of each run, Pallas kernels for 0% -> 0%
where the time goes in v1:
time: 232 us
  Pallas kernels  228 us (98%)
  local copies, waits for them, and re-layouts  3.61 us (2%)
    pallas_call x1, Pallas kernels, shards(): pl.pallas_call(kernel, out_shape=jax.ShapeDtypeStruct((2, TOK, Q), BF), i...  228 us

profile of v1, /device:TPU:1, one launch (start us, length us, event | category | flops | bytes accessed | tf_op | source)
XLA Modules:
  0.0 232.0 jit_solution(1576873006414372910)
XLA Ops:
  0.0 0.0 copy-start.1
  0.0 0.7 copy-done.1
  0.7 0.0 copy-start.2
  0.7 0.7 copy-done.2
  1.4 0.0 copy-start
  1.4 0.7 maximum_maximum_fusion.meta_in
  2.1 0.0 copy-done
  2.1 0.6 broadcast_in_dim.11.gain_in
  2.7 227.7 %shard_map.73 = bf16[2,64,512]{2,1,0:T(8,128)(2,1)} custom-call(bf16[2,64,512]{2,1,0:T(8,128)(2,1)} %tokens.1, f32[8,2048]{1,0:T(8,128)} %broadcast_in_dim.11.gain_in, f32[2,16,128]{2,1,0:T(8,128)} %maximum_maximum_fusion.meta_in, bf16[2048,256]{1,0:T(8,128)(2,1)} %bitcast.15, bf16[2048,256]{1,0:T(8,128)(2,1)} %bitcast.16, bf16[256,2048]{1,0:T(8,128)(2,1)} %bitcast.17), custom_call_target="tpu_custom_call" | custom-call | flops 3623878656 | bytes 8388608 | tf_op jit(solution)/shard_map/pallas_call | solution.py:493
  230.4 1.6 copy.9
  (1 shorter events, 0.0 us)
Async XLA Ops:
  0.0 0.7 copy-start.1
  0.7 0.7 copy-start.2
  1.4 0.7 copy-start

commit v2 on v0

v2 whole, which is shorter than its diff:
```python
import jax
import jax.numpy as jnp
from jax import lax
from jax.experimental import pallas as pl
from jax.experimental.pallas import tpu as pltpu
from jax.sharding import PartitionSpec as P

EPSILON = 1e-06
NZ, NY, NX = 16, 4, 4
TOK, TOPK, CAP = 64, 8, 9
D, Q, FFQ = 2048, 512, 256
ROWS = NZ * CAP
MESH = pl.DeviceIdType.MESH
PLACE = (0, 1, 15, 2, 14, 3, 13, 4, 12, 6, 10, 5, 11, 7, 9, 8)
AT = {distance: p for p, distance in enumerate(PLACE)}
PARENT = {
    3: (0, -3), 13: (0, 3), 2: (0, -2), 14: (0, 2), 1: (0, -1), 15: (0, 1),
    6: (3, -3), 4: (3, -1), 5: (3, -2), 10: (13, 3), 12: (13, 1),
    7: (6, -1), 8: (10, 2), 9: (10, 1), 11: (10, -1),
}
CHILDREN = {
    root: [child for child, (parent, _) in PARENT.items() if parent == root]
    for root in (0, 3, 13, 6, 10)
}
GROUPS = 3
PART = ROWS // GROUPS
PAIRS = tuple(range(g * PART // (2 * CAP), -(-(g + 1) * PART // (2 * CAP))) for g in range(GROUPS))
MIXES = tuple((q, g) for g in range(GROUPS) for q in PAIRS[g])
TURN = (0, 1, 3, 2)
WIDE = NY * PART
HALF = WIDE // 2
DIRECT = (False, False, False)
BF, F32 = jnp.bfloat16, jnp.float32

SCHEDULE = (
    "z 0", "z 13", "z 3", "zw 2", "zw 1", "zw 14", "zw 15", "b 2", "b 1", "b 0", "s 0", "w",
    "z 10", "xs 0 0", "z 6", "xs 0 1", "zw 4", "zw 12", "zw 5", "b 3", "b 5", "b 4", "s 1",
    "zw 11", "zw 8", "zw 9", "b 7", "zw 7", "b 6", "xp 0 0", "s 2", "xp 0 1", "xs 1 0",
    "xs 1 1", "xs 2 0", "xs 2 1", "e 0 1", "xp 1 1", "xp 2 0", "xp 1 0", "xp 2 1", "turn", "e 0 0",
    "f 0 1", "e 2 1", "e 2 0", "f 0 0", "e 1 1", "f 2 1", "e 1 0", "d 0 0", "f 2 0",
    "d 0 1", "f 1 1", "d 2 1", "f 1 0", "d 2 0", "r 0", "d 1 1", "c 1", "d 1 0", "r 2",
    "c 7", "c 6", "r 1", "c 3", "c 5", "c 4", "p 10", "p 6", "c 2", "c 0", "p 13", "p 3",
    "settle", "bn", "last",
)


def remote(src, dst, send, recv, device):
    return pltpu.make_async_remote_copy(
        src_ref=src,
        dst_ref=dst,
        send_sem=send,
        recv_sem=recv,
        device_id=device,
        device_id_type=MESH,
    )


def kernel(
    tokens,
    gain_in,
    named_in,
    weight_in,
    gate_in,
    up_in,
    down_in,
    out,
    gate,
    up,
    down,
    gains,
    blocks,
    named,
    weight,
    own_meta,
    meta,
    chosen,
    rows,
    parts,
    half,
    half_out,
    done,
    back,
    pick,
    mix,
    ring_out,
    ring_in,
    results,
    local_sem,
    pair_send,
    pair_recv,
    zg_send,
    zg_recv,
    zm_send,
    zm_recv,
    yg_send,
    yg_recv,
    yr_send,
    yr_recv,
    xg_send,
    xg_recv,
    xr_send,
    xr_recv,
    zr_send,
    zr_recv,
    turn,
):
    core = lax.axis_index("section")
    x = lax.axis_index("tp")
    ep = lax.axis_index("ep")
    z, y = ep // NY, ep % NY
    sibling = (1 - core, x, ep)

    def at_z(step):
        return (core, x, ((z + step + NZ) % NZ) * NY + y)

    def at_y(step):
        return (core, x, z * NY + (y + step + NY) % NY)

    x_one = x + 1 - 2 * (x % 2)
    x_three = 3 - x
    x_two = (x + 2) % 4
    quarter = (x, x_one, x_two, x_three)

    def at_x(which):
        return (core, which, ep)

    def pair_copies():
        sources = (
            (own_meta.at[1 - core], meta.at[0, core]),
            (gain_in, gains.at[core]),
            (gate_in, gate.at[core]),
            (up_in, up.at[core]),
            (down_in, down.at[core]),
        )
        return [
            remote(src, dst, pair_send.at[n], pair_recv.at[n], sibling)
            for n, (src, dst) in enumerate(sources)
        ]

    def own_copies():
        sources = (
            (tokens.at[core], blocks.at[0, 0]),
            (named_in, named),
            (weight_in, weight),
            (gain_in, gains.at[core]),
            (gate_in, gate.at[core]),
            (up_in, up.at[core]),
            (down_in, down.at[core]),
        )
        return [
            pltpu.make_async_copy(src, dst, local_sem.at[n]) for n, (src, dst) in enumerate(sources)
        ]

    pair, own = pair_copies(), own_copies()
    for copy in own:
        copy.start()

    barrier = pltpu.get_barrier_semaphore()
    friends = [sibling, at_y(1), at_y(2), at_y(3), at_x(x_one), at_x(x_three)]
    if any(DIRECT):
        friends += [at_x(x_two)]
    friends += [at_z(step) for step in (-3, -2, -1, 1, 2, 3)]
    for friend in friends:
        pl.semaphore_signal(barrier, inc=1, device_id=friend, device_id_type=MESH)
    own[1].wait()
    own[2].wait()
    for micro in range(2):
        entry = jnp.concatenate([named[micro].astype(F32), weight[micro]], axis=0)
        own_meta[micro] = jnp.concatenate([entry, entry], axis=1).astype(BF)
    meta[0, core] = own_meta[core]
    own[0].wait()
    pl.semaphore_wait(barrier, len(friends))

    for copy in pair:
        copy.start()

    def gather(layer, distance):
        parent, step = PARENT[distance]
        p = AT[distance]
        return remote(
            blocks.at[layer, AT[parent]],
            blocks.at[layer, p],
            zg_send.at[layer, p],
            zg_recv.at[layer, p],
            at_z(step),
        )

    def gather_meta(distance):
        parent, step = PARENT[distance]
        p = AT[distance]
        return remote(meta.at[AT[parent]], meta.at[p], zm_send.at[p], zm_recv.at[p], at_z(step))

    def reduce(layer, distance):
        _, step = PARENT[distance]
        p = AT[distance]
        return remote(
            ring_out.at[layer, p],
            ring_in.at[layer, p],
            zr_send.at[layer, p],
            zr_recv.at[layer, p],
            at_z(-step),
        )

    def y_go(layer, g, k):
        return remote(
            chosen.at[layer, g, pl.ds(k * PART, PART)],
            rows.at[layer, g, 0, pl.ds(k * PART, PART)],
            yg_send.at[layer, g, k],
            yg_recv.at[layer, g, k],
            at_y(TURN[k]),
        )

    def y_back(layer, g, k):
        return remote(
            done.at[layer, g, pl.ds(k * PART, PART)],
            back.at[layer, g, pl.ds(k * PART, PART)],
            yr_send.at[layer, g, k],
            yr_recv.at[layer, g, k],
            at_y(-TURN[k]),
        )

    def x_gather(layer, g, h):
        first, second = (1, 3) if h == 0 else (3, 1)
        span = pl.ds(h * HALF, HALF)
        source = 0 if DIRECT[g] else first
        far = 2 if DIRECT[g] else second
        return [
            remote(
                rows.at[layer, g, src, span],
                rows.at[layer, g, dst, span],
                xg_send.at[layer, g, h, n],
                xg_recv.at[layer, g, h, n],
                at_x(quarter[to]),
            )
            for n, (src, dst, to) in enumerate(
                ((0, first, first), (0, second, second), (source, 2, far))
            )
        ]

    def x_reduce(layer, g, h):
        first, second = (1, 3) if h == 0 else (3, 1)
        span = pl.ds(h * HALF, HALF)
        if DIRECT[g]:
            ways = [(parts.at[layer, g, n, span], n) for n in (2, 1, 3)]
        else:
            ways = [
                (parts.at[layer, g, 2, span], first),
                (parts.at[layer, g, first, span], first),
                (half_out.at[layer, g, span], second),
            ]
        return [
            remote(
                src,
                half.at[layer, g, n, span],
                xr_send.at[layer, g, h, n],
                xr_recv.at[layer, g, h, n],
                at_x(quarter[to]),
            )
            for n, (src, to) in enumerate(ways)
        ]

    def build_selection(layer, pairs):
        lane = lax.broadcasted_iota(jnp.int32, (2 * TOPK, 128), 1)
        low = lane < TOK
        a = lax.broadcasted_iota(jnp.int32, (128, 128), 0)
        b = lax.broadcasted_iota(jnp.int32, (128, 128), 1)
        before = jnp.where((a < b) & ((a < TOK) == (b < TOK)), 1.0, 0.0).astype(BF)
        row_number = lax.broadcasted_iota(jnp.int32, (PART, 128), 0).astype(F32)
        high_one = jnp.where(lax.broadcasted_iota(jnp.int32, (1, 128), 1) < TOK, 0.0, 1.0)
        for q in pairs:
            entry = jnp.where(
                low, meta[2 * q, layer].astype(F32), meta[2 * q + 1, layer].astype(F32)
            )
            named, weight = entry[:TOPK], entry[TOPK:]
            same = [
                jnp.where(named == (z * NY + (y + TURN[k]) % NY).astype(F32), 1.0, 0.0)
                for k in range(NY)
            ]
            count = jnp.dot(
                jnp.concatenate(same, axis=0).astype(BF), before, preferred_element_type=F32
            )
            for k in range(NY):
                position = jnp.sum(count[k * TOPK : (k + 1) * TOPK], axis=0, keepdims=True)
                hits = jnp.sum(same[k], axis=0, keepdims=True)
                share = jnp.sum(same[k] * weight, axis=0, keepdims=True)
                slot = jnp.where(hits > 0.5, position + CAP * (2 * q + high_one), -1.0)
                for m, (other, g) in enumerate(MIXES):
                    if other == q:
                        hit = row_number + g * PART == slot
                        at = (q - PAIRS[g][0]) * 128
                        pick[layer, g, k * PART : (k + 1) * PART, at : at + 128] = jnp.where(
                            hit, 1.0, 0.0
                        ).astype(BF)
                        mix[layer, m, k * PART : (k + 1) * PART, :] = jnp.where(
                            hit, share, 0.0
                        ).astype(BF)

    def expert(layer, g, h):
        span_rows = slice(h * HALF, (h + 1) * HALF)
        total = jnp.zeros((HALF, 1), F32)
        for s in range(4):
            value = rows[layer, g, s, span_rows].astype(F32)
            total = total + jnp.sum(value * value, axis=1, keepdims=True)
        scale = lax.rsqrt(total / D + EPSILON)
        gate_act = jnp.zeros((HALF, FFQ), F32)
        up_act = jnp.zeros((HALF, FFQ), F32)
        for s in range(4):
            span = pl.ds(pl.multiple_of(quarter[s] * Q, Q), Q)
            value = rows[layer, g, s, span_rows].astype(F32)
            normed = (value * scale * gains[layer, 0:1, span]).astype(BF)
            gate_act += jnp.dot(normed, gate[layer, span, :], preferred_element_type=F32)
            up_act += jnp.dot(normed, up[layer, span, :], preferred_element_type=F32)
        hidden = (gate_act / (1.0 + jnp.exp(-gate_act)) * up_act).astype(BF)
        sends = x_reduce(layer, g, h)
        first = 1 if h == 0 else 3
        order = (2, 1, 3, 0) if DIRECT[g] else (2, first, 4 - first, 0)
        for n, s in enumerate(order):
            span = pl.ds(pl.multiple_of(quarter[s] * Q, Q), Q)
            parts[layer, g, s, span_rows] = jnp.dot(
                hidden, down[layer, :, span], preferred_element_type=F32
            ).astype(BF)
            if n < (3 if DIRECT[g] else 2):
                sends[n].start()

    def one_layer(layer, carry):
        sums = {}

        def first_only(action):
            pl.when(layer == 0)(action)

        def z_pass(root):
            if root:
                gather(layer, root).wait_recv()
            for distance in CHILDREN[root]:
                gather(layer, distance).start()

            @first_only
            def _():
                if root:
                    gather_meta(root).wait_recv()
                else:
                    pair[0].wait()
                for distance in CHILDREN[root]:
                    gather_meta(distance).start()

        def z_wait(*distances):
            for distance in distances:
                gather(layer, distance).wait_recv()

            @first_only
            def _():
                for distance in distances:
                    gather_meta(distance).wait_recv()

        def build(*pairs):
            first_only(lambda: build_selection(0, pairs))

        def build_next():
            first_only(lambda: build_selection(1, range(NZ // 2)))

        def select(g):
            pairs = PAIRS[g]
            source = blocks[layer, 2 * pairs[0] : 2 * pairs[-1] + 2].reshape(-1, Q)
            value = jnp.dot(
                pick[layer, g, :, 0 : len(pairs) * 128], source, preferred_element_type=F32
            ).astype(BF)
            chosen[layer, g] = value
            for k in (1, 2, 3):
                y_go(layer, g, k).start()
            rows[layer, g, 0, 0:PART] = value[:PART]

        def x_send(g, h):
            for k in (2 * h, 2 * h + 1):
                if k:
                    y_go(layer, g, k).wait_recv()
            copies = x_gather(layer, g, h)
            for copy in copies if DIRECT[g] else copies[:2]:
                copy.start()

        def x_pass(g, h):
            copies = x_gather(layer, g, h)
            copies[0].wait_recv()
            if not DIRECT[g]:
                copies[2].start()

        def weights():
            @first_only
            def _():
                for copy in pair[1:] + own[3:]:
                    copy.wait()

        def work(g, h):
            copies = x_gather(layer, g, h)
            copies[1].wait_recv()
            copies[2].wait_recv()
            expert(layer, g, h)

        def fold(g, h):
            if not DIRECT[g]:
                span = slice(h * HALF, (h + 1) * HALF)
                copies = x_reduce(layer, g, h)
                copies[0].wait_recv()
                half_out[layer, g, span] = (
                    parts[layer, g, 3 - 2 * h, span].astype(F32)
                    + half[layer, g, 0, span].astype(F32)
                ).astype(BF)
                copies[2].start()

        def finish(g, h):
            span = slice(h * HALF, (h + 1) * HALF)
            copies = x_reduce(layer, g, h)
            terms = (0, 1, 2) if DIRECT[g] else (1, 2)
            for n in terms:
                copies[n].wait_recv()
            value = parts[layer, g, 0, span].astype(F32)
            for n in terms:
                value = value + half[layer, g, n, span].astype(F32)
            value = value.astype(BF)
            done[layer, g, span] = value
            for k in (2 * h, 2 * h + 1):
                if k:
                    y_back(layer, g, k).start()
            if h == 0:
                back[layer, g, 0:PART] = value[:PART]

        def returned(g):
            for k in (1, 2, 3):
                y_back(layer, g, k).wait_recv()

        def collect(distance, value):
            for child in CHILDREN.get(distance, ()):
                reduce(layer, child).wait_recv()
                value = value + ring_in[layer, AT[child]].astype(F32)
            return value

        def pass_on(distance):
            ring_out[layer, AT[distance]] = collect(distance, sums[distance]).astype(BF)
            reduce(layer, distance).start()

        def combine(q):
            value = None
            for m, (other, g) in enumerate(MIXES):
                if other == q:
                    term = lax.dot_general(
                        mix[layer, m],
                        back[layer, g],
                        (((0,), (0,)), ((), ())),
                        preferred_element_type=F32,
                    )
                    value = term if value is None else value + term
            for k in range(2):
                distance = PLACE[2 * q + k]
                sums[distance] = value[k * TOK : (k + 1) * TOK]
                if distance not in CHILDREN:
                    pass_on(distance)

        def settle():
            for distance in PLACE[1:]:
                gather(layer, distance).wait_send()
                if distance not in (3, 13):
                    reduce(layer, distance).wait_send()

            @first_only
            def _():
                for distance in PLACE[1:]:
                    gather_meta(distance).wait_send()

            for g in range(GROUPS):
                for k in (1, 2, 3):
                    y_go(layer, g, k).wait_send()
                    y_back(layer, g, k).wait_send()
                for h in range(2):
                    for copy in x_gather(layer, g, h) + x_reduce(layer, g, h):
                        copy.wait_send()

        def last():
            for distance in (3, 13):
                reduce(layer, distance).wait_send()
            final = collect(0, sums[0] + blocks[layer, 0].astype(F32)).astype(BF)
            results[layer] = final

            @first_only
            def _():
                blocks[1, 0] = final

        steps = dict(
            z=z_pass, zw=z_wait, b=build, bn=build_next, s=select, xs=x_send, xp=x_pass,
            w=weights, e=work, f=fold, d=finish, r=returned, c=combine, p=pass_on,
            settle=settle, last=last,
        )
        @pl.when((layer == 0) & (core == 1))
        def _():
            pl.semaphore_wait(turn, 1)

        def hand_over():
            @pl.when((layer == 0) & (core == 0))
            def _():
                pl.semaphore_signal(turn, inc=1, device_id=sibling, device_id_type=MESH)

        steps["turn"] = hand_over
        for step in SCHEDULE:
            name, *places = step.split()
            steps[name](*[int(place) for place in places])
        return carry

    lax.fori_loop(0, 2, one_layer, 0)
    last = remote(results.at[1 - core], out.at[core], pair_send.at[5], pair_recv.at[5], sibling)
    last.start()
    keep = pltpu.make_async_copy(results.at[core], out.at[core], local_sem.at[0])
    keep.start()
    keep.wait()
    last.wait()


def shards(tokens, norm_gain, expert_gate, expert_up, expert_down, routes, route_weights):
    named = jnp.swapaxes(routes[0], 1, 2)
    weight = jnp.swapaxes(route_weights[0], 1, 2)
    anywhere = pl.BlockSpec(memory_space=pl.ANY)
    dma = pltpu.SemaphoreType.DMA
    out = pl.pallas_call(
        kernel,
        out_shape=jax.ShapeDtypeStruct((2, TOK, Q), BF),
        in_specs=[anywhere] * 7,
        out_specs=anywhere,
        scratch_shapes=[
            pltpu.VMEM((2, D, FFQ), BF),
            pltpu.VMEM((2, D, FFQ), BF),
            pltpu.VMEM((2, FFQ, D), BF),
            pltpu.VMEM((2, 1, D), F32),
            pltpu.VMEM((2, NZ, TOK, Q), BF),
            pltpu.VMEM((2, TOPK, TOK), jnp.int32),
            pltpu.VMEM((2, TOPK, TOK), F32),
            pltpu.VMEM((2, 2 * TOPK, 128), BF),
            pltpu.VMEM((NZ, 2, 2 * TOPK, 128), BF),
            pltpu.VMEM((2, GROUPS, WIDE, Q), BF),
            pltpu.VMEM((2, GROUPS, 4, WIDE, Q), BF),
            pltpu.VMEM((2, GROUPS, 4, WIDE, Q), BF),
            pltpu.VMEM((2, GROUPS, 3, WIDE, Q), BF),
            pltpu.VMEM((2, GROUPS, WIDE, Q), BF),
            pltpu.VMEM((2, GROUPS, WIDE, Q), BF),
            pltpu.VMEM((2, GROUPS, WIDE, Q), BF),
            pltpu.VMEM((2, GROUPS, WIDE, 512), BF),
            pltpu.VMEM((2, len(MIXES), WIDE, 128), BF),
            pltpu.VMEM((2, NZ, TOK, Q), BF),
            pltpu.VMEM((2, NZ, TOK, Q), BF),
            pltpu.VMEM((2, TOK, Q), BF),
            dma((7,)),
            dma((6,)),
            dma((6,)),
            dma((2, NZ)),
            dma((2, NZ)),
            dma((NZ,)),
            dma((NZ,)),
            dma((2, GROUPS, NY)),
            dma((2, GROUPS, NY)),
            dma((2, GROUPS, NY)),
            dma((2, GROUPS, NY)),
            dma((2, GROUPS, 2, 3)),
            dma((2, GROUPS, 2, 3)),
            dma((2, GROUPS, 2, 3)),
            dma((2, GROUPS, 2, 3)),
            dma((2, NZ)),
            dma((2, NZ)),
            pltpu.SemaphoreType.REGULAR,
        ],
        compiler_params=pltpu.CompilerParams(
            collective_id=0, has_side_effects=True, vmem_limit_bytes=56 * 1024 * 1024
        ),
        cost_estimate=pl.CostEstimate(
            flops=2 * 2 * 576 * D * 768, bytes_accessed=8 * 1024 * 1024, transcendentals=0
        ),
    )(tokens, norm_gain, named, weight, expert_gate[0, 0], expert_up[0, 0], expert_down[0, 0])
    return out[None]


def solution(mesh):
    placed = (
        P(None, "ep", "tp"),
        P("section", None),
        P("section", "ep", None, "tp"),
        P("section", "ep", None, "tp"),
        P("section", "ep", "tp", None),
        P("section", None, "ep", None),
        P("section", None, "ep", None),
    )
    return jax.shard_map(
        shards,
        mesh=mesh,
        in_specs=placed,
        out_specs=P("section", None, "ep", "tp"),
        check_vma=False,
    )
```

time: 749 us -> 166 us (0.22)
  waiting for transfers between devices: 310 us -> 0 us
  blocking collectives: 295 us -> 0 us
  Pallas kernels: 0 us -> 164 us
  starting transfers between devices: 48.8 us -> 0 us
  local copies, waits for them, and re-layouts: 35.7 us -> 1.57 us
  matrix products: 28.5 us -> 0 us
  between operations: 13.7 us -> 0.01 us
  other arithmetic: 12.7 us -> 0 us
    all_to_all x6 -> x0, blocking collectives: 272 us -> none  [the longest x3 179 us: shards(): lax.all_to_all(buffer.reshape(expert_count, capacity, quarter), 'ep', spl...]
    pallas_call x0 -> x1, Pallas kernels: none -> 164 us  [shards(): pl.pallas_call(kernel, out_shape=jax.ShapeDtypeStruct((2, TOK, Q), BF), i...]
    all_gather x3 -> x0, waiting for transfers between devices: 154 us -> none  [shards(): shard_part = lax.all_gather(arrived, 'tp', axis=2, tiled=True)]
    all_to_all x3 -> x0, waiting for transfers between devices: 144 us -> none  [shards(): lax.all_to_all(expert_out.reshape(expert_count, capacity, quarter), 'ep',...]
    all_to_all x3 -> x0, starting transfers between devices: 46.1 us -> none  [shards(): lax.all_to_all(expert_out.reshape(expert_count, capacity, quarter), 'ep',...]
    dot_general x12 -> x0, matrix products: 28.5 us -> none  [the longest x3 16.1 us: shards(): jnp.dot(hidden, weight_down, preferred_element_type=jnp.float32)]
    reshape x15 -> x0, local copies, waits for them, and re-layouts: 23.7 us -> none  [the longest x3 10.1 us: shards(): rows_part = shard_part.reshape(slot_total, feature_count)]
    psum x3 -> x0, blocking collectives: 23.1 us -> none  [shards(): square_sum = lax.psum(jnp.sum(values * values, axis=1), 'tp')]
  transfers between devices with their start and end apart: 8 -> 0, of which waited for: 8 -> 0; matrix products, arithmetic and copies ran while one was open for 1% -> 0% of each run, Pallas kernels for 0% -> 0%
where the time goes in v2:
time: 166 us
  Pallas kernels  164 us (99%)
    pallas_call x1, Pallas kernels, shards(): pl.pallas_call(kernel, out_shape=jax.ShapeDtypeStruct((2, TOK, Q), BF), i...  164 us

profile of v2, /device:TPU:1, one launch (start us, length us, event | category | flops | bytes accessed | tf_op | source)
XLA Modules:
  0.0 165.8 jit_solution(3120257476438983011)
XLA Ops:
  0.0 164.3 %shard_map.73 = bf16[2,64,512]{2,1,0:T(8,128)(2,1)} custom-call(bf16[2,64,512]{2,1,0:T(8,128)(2,1)} %tokens.1, f32[1,2048]{1,0:T(1,128)} %gain_in.1, s32[2,8,64]{2,1,0:T(8,128)} %bitcast.14, f32[2,8,64]{2,1,0:T(8,128)} %bitcast.15, bf16[2048,256]{1,0:T(8,128)(2,1)} %bitcast.11, bf16[2048,256]{1,0:T(8,128)(2,1)} %bitcast.12, bf16[256,2048]{1,0:T(8,128)(2,1)} %bitcast.13), custom_call_target="tpu_custom_call" | custom-call | flops 3623878656 | bytes 8388608 | tf_op jit(solution)/shard_map/pallas_call | solution.py:520
  164.3 1.6 copy.9

commit v3 on v2

--- a/solution.py
+++ b/solution.py
@@ -29,18 +29,18 @@
 TURN = (0, 1, 3, 2)
 WIDE = NY * PART
 HALF = WIDE // 2
-DIRECT = (False, False, False)
+DIRECT = (False, False, True)
 BF, F32 = jnp.bfloat16, jnp.float32
 
 SCHEDULE = (
-    "z 0", "z 13", "z 3", "zw 2", "zw 1", "zw 14", "zw 15", "b 2", "b 1", "b 0", "s 0", "w",
-    "z 10", "xs 0 0", "z 6", "xs 0 1", "zw 4", "zw 12", "zw 5", "b 3", "b 5", "b 4", "s 1",
-    "zw 11", "zw 8", "zw 9", "b 7", "zw 7", "b 6", "xp 0 0", "s 2", "xp 0 1", "xs 1 0",
-    "xs 1 1", "xs 2 0", "xs 2 1", "e 0 1", "xp 1 1", "xp 2 0", "xp 1 0", "xp 2 1", "turn", "e 0 0",
-    "f 0 1", "e 2 1", "e 2 0", "f 0 0", "e 1 1", "f 2 1", "e 1 0", "d 0 0", "f 2 0",
-    "d 0 1", "f 1 1", "d 2 1", "f 1 0", "d 2 0", "r 0", "d 1 1", "c 1", "d 1 0", "r 2",
-    "c 7", "c 6", "r 1", "c 3", "c 5", "c 4", "p 10", "p 6", "c 2", "c 0", "p 13", "p 3",
-    "settle", "bn", "last",
+    "hold", "z 0", "z 13", "z 3", "zw 14", "zw 15", "zw 1", "b 2", "zw 2", "b 0", "b 1",
+    "s 0", "z 10", "z 6", "zw 12", "zw 4", "xs 0 0", "b 3", "zw 5", "b 4", "b 5", "s 1",
+    "xs 0 1", "zw 11", "zw 8", "zw 7", "w", "b 6", "zw 9", "b 7", "s 2", "xs 1 0", "xp 0 0",
+    "xp 0 1", "xs 1 1", "xs 2 1", "bn", "xp 1 0", "xp 1 1", "xs 2 0", "xp 2 1", "e 2 1",
+    "e 1 0", "turn", "e 1 1", "f 2 1", "xp 2 0", "e 2 0", "f 2 0", "d 2 1", "f 1 0",
+    "f 1 1", "e 0 1", "e 0 0", "d 2 0", "d 1 1", "d 1 0", "f 0 1", "f 0 0", "r 2", "c 7",
+    "c 6", "r 1", "c 3", "d 0 1", "c 5", "d 0 0", "c 4", "p 6", "p 10", "r 0", "c 0", "c 1",
+    "c 2", "p 3", "p 13", "settle", "last",
 )
 
 
@@ -322,6 +322,9 @@
             if n < (3 if DIRECT[g] else 2):
                 sends[n].start()
 
+    across = remote(results.at[1 - core], out.at[core], pair_send.at[5], pair_recv.at[5], sibling)
+    keep = pltpu.make_async_copy(results.at[core], out.at[core], local_sem.at[0])
+
     def one_layer(layer, carry):
         sums = {}
 
@@ -483,14 +486,18 @@
             def _():
                 blocks[1, 0] = final
 
+            pl.when(layer == core)(keep.start)
+            pl.when(layer != core)(across.start)
+
         steps = dict(
             z=z_pass, zw=z_wait, b=build, bn=build_next, s=select, xs=x_send, xp=x_pass,
             w=weights, e=work, f=fold, d=finish, r=returned, c=combine, p=pass_on,
             settle=settle, last=last,
         )
-        @pl.when((layer == 0) & (core == 1))
-        def _():
-            pl.semaphore_wait(turn, 1)
+        def hold():
+            @pl.when((layer == 0) & (core == 1))
+            def _():
+                pl.semaphore_wait(turn, 1)
 
         def hand_over():
             @pl.when((layer == 0) & (core == 0))
@@ -498,18 +505,15 @@
                 pl.semaphore_signal(turn, inc=1, device_id=sibling, device_id_type=MESH)
 
         steps["turn"] = hand_over
+        steps["hold"] = hold
         for step in SCHEDULE:
             name, *places = step.split()
             steps[name](*[int(place) for place in places])
         return carry
 
     lax.fori_loop(0, 2, one_layer, 0)
-    last = remote(results.at[1 - core], out.at[core], pair_send.at[5], pair_recv.at[5], sibling)
-    last.start()
-    keep = pltpu.make_async_copy(results.at[core], out.at[core], local_sem.at[0])
-    keep.start()
+    across.wait()
     keep.wait()
-    last.wait()
 
 
 def shards(tokens, norm_gain, expert_gate, expert_up, expert_down, routes, route_weights):

time: 166 us -> 159 us (0.958)
  Pallas kernels: 164 us -> 157 us
    pallas_call x1, Pallas kernels: 164 us -> 157 us  [shards(): pl.pallas_call(kernel, out_shape=jax.ShapeDtypeStruct((2, TOK, Q), BF), i...]
where the time goes in v3:
time: 159 us
  Pallas kernels  157 us (99%)
    pallas_call x1, Pallas kernels, shards(): pl.pallas_call(kernel, out_shape=jax.ShapeDtypeStruct((2, TOK, Q), BF), i...  157 us

profile of v3, /device:TPU:1, one launch (start us, length us, event | category | flops | bytes accessed | tf_op | source)
XLA Modules:
  0.0 159.0 jit_solution(4184885694176319455)
XLA Ops:
  0.0 157.4 %shard_map.73 = bf16[2,64,512]{2,1,0:T(8,128)(2,1)} custom-call(bf16[2,64,512]{2,1,0:T(8,128)(2,1)} %tokens.1, f32[1,2048]{1,0:T(1,128)} %gain_in.1, s32[2,8,64]{2,1,0:T(8,128)} %bitcast.14, f32[2,8,64]{2,1,0:T(8,128)} %bitcast.15, bf16[2048,256]{1,0:T(8,128)(2,1)} %bitcast.11, bf16[2048,256]{1,0:T(8,128)(2,1)} %bitcast.12, bf16[256,2048]{1,0:T(8,128)(2,1)} %bitcast.13), custom_call_target="tpu_custom_call" | custom-call | flops 3623878656 | bytes 8388608 | tf_op jit(solution)/shard_map/pallas_call | solution.py:524
  157.4 1.6 copy.9

commit v4 on v3

--- a/solution.py
+++ b/solution.py
@@ -29,18 +29,20 @@
 TURN = (0, 1, 3, 2)
 WIDE = NY * PART
 HALF = WIDE // 2
+PIECES = 2
+PIECE = TOK // PIECES
 DIRECT = (False, False, True)
 BF, F32 = jnp.bfloat16, jnp.float32
 
 SCHEDULE = (
-    "hold", "z 0", "z 13", "z 3", "zw 14", "zw 15", "zw 1", "b 2", "zw 2", "b 0", "b 1",
-    "s 0", "z 10", "z 6", "zw 12", "zw 4", "xs 0 0", "b 3", "zw 5", "b 4", "b 5", "s 1",
-    "xs 0 1", "zw 11", "zw 8", "zw 7", "w", "b 6", "zw 9", "b 7", "s 2", "xs 1 0", "xp 0 0",
-    "xp 0 1", "xs 1 1", "xs 2 1", "bn", "xp 1 0", "xp 1 1", "xs 2 0", "xp 2 1", "e 2 1",
-    "e 1 0", "turn", "e 1 1", "f 2 1", "xp 2 0", "e 2 0", "f 2 0", "d 2 1", "f 1 0",
-    "f 1 1", "e 0 1", "e 0 0", "d 2 0", "d 1 1", "d 1 0", "f 0 1", "f 0 0", "r 2", "c 7",
-    "c 6", "r 1", "c 3", "d 0 1", "c 5", "d 0 0", "c 4", "p 6", "p 10", "r 0", "c 0", "c 1",
-    "c 2", "p 3", "p 13", "settle", "last",
+    "hold", "z 0", "z 3 13", "zw 14", "zw 15", "zw 1", "b 2", "zw 2", "b 0", "b 1", "s 0",
+    "z 6 10", "zw 12", "zw 4", "xs 0 0", "b 3", "zw 5", "b 4", "b 5", "s 1", "xs 0 1",
+    "zw 11", "zw 8", "zw 7", "w", "b 6", "zw 9", "b 7", "s 2", "xs 1 0", "xp 0 0", "xp 0 1",
+    "xs 1 1", "xs 2 1", "bn", "xp 1 0", "xp 1 1", "xs 2 0", "xp 2 1", "e 2 1", "e 1 0",
+    "e 1 1", "turn", "f 2 1", "xp 2 0", "e 2 0", "f 2 0", "d 2 1", "f 1 0", "f 1 1",
+    "e 0 1", "e 0 0", "d 2 0", "d 1 1", "d 1 0", "f 0 1", "f 0 0", "r 2", "c 7", "c 6",
+    "r 1", "c 3", "d 0 1", "c 5", "d 0 0", "c 4", "p 6 10", "r 0", "c 0", "c 1", "c 2",
+    "p 3 13", "settle", "last",
 )
 
 
@@ -174,14 +176,15 @@
     for copy in pair:
         copy.start()
 
-    def gather(layer, distance):
+    def gather(layer, distance, piece):
         parent, step = PARENT[distance]
         p = AT[distance]
+        span = pl.ds(piece * PIECE, PIECE)
         return remote(
-            blocks.at[layer, AT[parent]],
-            blocks.at[layer, p],
-            zg_send.at[layer, p],
-            zg_recv.at[layer, p],
+            blocks.at[layer, AT[parent], span],
+            blocks.at[layer, p, span],
+            zg_send.at[layer, p, piece],
+            zg_recv.at[layer, p, piece],
             at_z(step),
         )
 
@@ -190,14 +193,15 @@
         p = AT[distance]
         return remote(meta.at[AT[parent]], meta.at[p], zm_send.at[p], zm_recv.at[p], at_z(step))
 
-    def reduce(layer, distance):
+    def reduce(layer, distance, piece):
         _, step = PARENT[distance]
         p = AT[distance]
+        span = pl.ds(piece * PIECE, PIECE)
         return remote(
-            ring_out.at[layer, p],
-            ring_in.at[layer, p],
-            zr_send.at[layer, p],
-            zr_recv.at[layer, p],
+            ring_out.at[layer, p, span],
+            ring_in.at[layer, p, span],
+            zr_send.at[layer, p, piece],
+            zr_recv.at[layer, p, piece],
             at_z(-step),
         )
 
@@ -331,24 +335,32 @@
         def first_only(action):
             pl.when(layer == 0)(action)
 
-        def z_pass(root):
-            if root:
-                gather(layer, root).wait_recv()
-            for distance in CHILDREN[root]:
-                gather(layer, distance).start()
+        def z_pass(*roots):
+            if roots == (0,):
+                for distance in CHILDREN[0]:
+                    for piece in range(PIECES):
+                        gather(layer, distance, piece).start()
+            else:
+                for piece in range(PIECES):
+                    for root in roots:
+                        gather(layer, root, piece).wait_recv()
+                        for distance in CHILDREN[root]:
+                            gather(layer, distance, piece).start()
 
             @first_only
             def _():
-                if root:
-                    gather_meta(root).wait_recv()
-                else:
-                    pair[0].wait()
-                for distance in CHILDREN[root]:
-                    gather_meta(distance).start()
+                for root in roots:
+                    if root:
+                        gather_meta(root).wait_recv()
+                    else:
+                        pair[0].wait()
+                    for distance in CHILDREN[root]:
+                        gather_meta(distance).start()
 
         def z_wait(*distances):
             for distance in distances:
-                gather(layer, distance).wait_recv()
+                for piece in range(PIECES):
+                    gather(layer, distance, piece).wait_recv()
 
             @first_only
             def _():
@@ -430,15 +442,20 @@
             for k in (1, 2, 3):
                 y_back(layer, g, k).wait_recv()
 
-        def collect(distance, value):
+        def collect(distance, piece, value):
             for child in CHILDREN.get(distance, ()):
-                reduce(layer, child).wait_recv()
-                value = value + ring_in[layer, AT[child]].astype(F32)
+                reduce(layer, child, piece).wait_recv()
+                span = slice(piece * PIECE, (piece + 1) * PIECE)
+                value = value + ring_in[layer, AT[child], span].astype(F32)
             return value
 
-        def pass_on(distance):
-            ring_out[layer, AT[distance]] = collect(distance, sums[distance]).astype(BF)
-            reduce(layer, distance).start()
+        def pass_on(*distances):
+            for piece in range(PIECES):
+                span = slice(piece * PIECE, (piece + 1) * PIECE)
+                for distance in distances:
+                    value = collect(distance, piece, sums[distance][span])
+                    ring_out[layer, AT[distance], span] = value.astype(BF)
+                    reduce(layer, distance, piece).start()
 
         def combine(q):
             value = None
@@ -459,9 +476,10 @@
 
         def settle():
             for distance in PLACE[1:]:
-                gather(layer, distance).wait_send()
-                if distance not in (3, 13):
-                    reduce(layer, distance).wait_send()
+                for piece in range(PIECES):
+                    gather(layer, distance, piece).wait_send()
+                    if distance not in (3, 13):
+                        reduce(layer, distance, piece).wait_send()
 
             @first_only
             def _():
@@ -477,14 +495,18 @@
                         copy.wait_send()
 
         def last():
-            for distance in (3, 13):
-                reduce(layer, distance).wait_send()
-            final = collect(0, sums[0] + blocks[layer, 0].astype(F32)).astype(BF)
-            results[layer] = final
-
-            @first_only
-            def _():
-                blocks[1, 0] = final
+            for piece in range(PIECES):
+                span = slice(piece * PIECE, (piece + 1) * PIECE)
+                value = sums[0][span] + blocks[layer, 0, span].astype(F32)
+                final = collect(0, piece, value).astype(BF)
+                results[layer, span] = final
+
+                @first_only
+                def _():
+                    blocks[1, 0, span] = final
+
+                for distance in (3, 13):
+                    reduce(layer, distance, piece).wait_send()
 
             pl.when(layer == core)(keep.start)
             pl.when(layer != core)(across.start)
@@ -551,8 +573,8 @@
             dma((7,)),
             dma((6,)),
             dma((6,)),
-            dma((2, NZ)),
-            dma((2, NZ)),
+            dma((2, NZ, PIECES)),
+            dma((2, NZ, PIECES)),
             dma((NZ,)),
             dma((NZ,)),
             dma((2, GROUPS, NY)),
@@ -563,8 +585,8 @@
             dma((2, GROUPS, 2, 3)),
             dma((2, GROUPS, 2, 3)),
             dma((2, GROUPS, 2, 3)),
-            dma((2, NZ)),
-            dma((2, NZ)),
+            dma((2, NZ, PIECES)),
+            dma((2, NZ, PIECES)),
             pltpu.SemaphoreType.REGULAR,
         ],
         compiler_params=pltpu.CompilerParams(

time: 159 us -> 156 us (0.981)
  Pallas kernels: 157 us -> 154 us
    pallas_call x1, Pallas kernels: 157 us -> 154 us  [shards(): pl.pallas_call(kernel, out_shape=jax.ShapeDtypeStruct((2, TOK, Q), BF), i...]
where the time goes in v4:
time: 156 us
  Pallas kernels  154 us (99%)
  local copies, waits for them, and re-layouts  1.57 us (1%)
    pallas_call x1, Pallas kernels, shards(): pl.pallas_call(kernel, out_shape=jax.ShapeDtypeStruct((2, TOK, Q), BF), i...  154 us

profile of v4, /device:TPU:1, one launch (start us, length us, event | category | flops | bytes accessed | tf_op | source)
XLA Modules:
  0.0 155.7 jit_solution(8955514881226499010)
XLA Ops:
  0.0 154.1 %shard_map.73 = bf16[2,64,512]{2,1,0:T(8,128)(2,1)} custom-call(bf16[2,64,512]{2,1,0:T(8,128)(2,1)} %tokens.1, f32[1,2048]{1,0:T(1,128)} %gain_in.1, s32[2,8,64]{2,1,0:T(8,128)} %bitcast.14, f32[2,8,64]{2,1,0:T(8,128)} %bitcast.15, bf16[2048,256]{1,0:T(8,128)(2,1)} %bitcast.11, bf16[2048,256]{1,0:T(8,128)(2,1)} %bitcast.12, bf16[256,2048]{1,0:T(8,128)(2,1)} %bitcast.13), custom_call_target="tpu_custom_call" | custom-call | flops 3623878656 | bytes 8388608 | tf_op jit(solution)/shard_map/pallas_call | solution.py:546
  154.1 1.6 %copy.9 = bf16[1,2,64,512]{3,2,1,0:T(8,128)(2,1)} copy(bf16[1,2,64,512]{3,2,1,0:T(8,128)(2,1)} %bitcast.10) | data formatting | bytes 262144

commit v5 on v4

--- a/solution.py
+++ b/solution.py
@@ -39,7 +39,7 @@
     "z 6 10", "zw 12", "zw 4", "xs 0 0", "b 3", "zw 5", "b 4", "b 5", "s 1", "xs 0 1",
     "zw 11", "zw 8", "zw 7", "w", "b 6", "zw 9", "b 7", "s 2", "xs 1 0", "xp 0 0", "xp 0 1",
     "xs 1 1", "xs 2 1", "bn", "xp 1 0", "xp 1 1", "xs 2 0", "xp 2 1", "e 2 1", "e 1 0",
-    "e 1 1", "turn", "f 2 1", "xp 2 0", "e 2 0", "f 2 0", "d 2 1", "f 1 0", "f 1 1",
+    "e 1 1", "f 2 1", "xp 2 0", "turn", "e 2 0", "f 2 0", "d 2 1", "f 1 0", "f 1 1",
     "e 0 1", "e 0 0", "d 2 0", "d 1 1", "d 1 0", "f 0 1", "f 0 0", "r 2", "c 7", "c 6",
     "r 1", "c 3", "d 0 1", "c 5", "d 0 0", "c 4", "p 6 10", "r 0", "c 0", "c 1", "c 2",
     "p 3 13", "settle", "last",

time: 156 us -> 157 us (level)
  Pallas kernels: 154 us -> 156 us
where the time goes in v5:
time: 157 us
  Pallas kernels  156 us (99%)
  local copies, waits for them, and re-layouts  1.57 us (1%)
    pallas_call x1, Pallas kernels, shards(): pl.pallas_call(kernel, out_shape=jax.ShapeDtypeStruct((2, TOK, Q), BF), i...  156 us

profile of v5, /device:TPU:1, one launch (start us, length us, event | category | flops | bytes accessed | tf_op | source)
XLA Modules:
  0.0 157.2 jit_solution(9802776096489966193)
XLA Ops:
  0.0 155.6 %shard_map.73 = bf16[2,64,512]{2,1,0:T(8,128)(2,1)} custom-call(bf16[2,64,512]{2,1,0:T(8,128)(2,1)} %tokens.1, f32[1,2048]{1,0:T(1,128)} %gain_in.1, s32[2,8,64]{2,1,0:T(8,128)} %bitcast.14, f32[2,8,64]{2,1,0:T(8,128)} %bitcast.15, bf16[2048,256]{1,0:T(8,128)(2,1)} %bitcast.11, bf16[2048,256]{1,0:T(8,128)(2,1)} %bitcast.12, bf16[256,2048]{1,0:T(8,128)(2,1)} %bitcast.13), custom_call_target="tpu_custom_call" | custom-call | flops 3623878656 | bytes 8388608 | tf_op jit(solution)/shard_map/pallas_call | solution.py:546
  155.6 1.6 copy.9
